TPU v7x, 512 devices: a whole 4x4x16 slice. The times are simulated.
512 devices in a mesh: row: 16 (over y, x), col: 32 (over z, core).
Axes of the slice: x: 4, y: 4, z: 16, core: 2. Of those that a mesh axis runs over, the one named last changes fastest.
Arguments:
- tokens: bfloat16 [512, 12288], P('col', 'row'), may hold values from -6 to 6
- up_proj: bfloat16 [12288, 24576], P('row', 'col'), may hold values from -0.109375 to 0.109375
- down_proj: bfloat16 [24576, 12288], P('col', 'row'), may hold values from -0.078125 to 0.078125
- keep_mask: int32 [96, 192], P('row', 'col'), may hold values from 0 to 1, as said below
- cotangent: bfloat16 [512, 12288], P('col', 'row'), may hold values from -3 to 3
Outputs:
- output: bfloat16 [512, 12288], P('col', 'row')
- input_grad: bfloat16 [512, 12288], P('col', 'row')
- up_grad: bfloat16 [12288, 24576], P('row', 'col')
- down_grad: bfloat16 [24576, 12288], P('col', 'row')
Inputs may be any that keep to these rules, and one draw needn't show every extreme that they name: `keep_mask`: the device grid cuts the mask into tiles of (12288 / 128 / 16) x (24576 / 128 / 32) blocks, split as up_proj; a tile keeps at most 24 blocks and some tile keeps exactly 24; tiles may keep none.
All inputs are finite; a program needn't handle non-finite values.
Results may differ from a plain program's by a relative error of at most 0.034.
Values may be sent and summed in bfloat16 or wider, within the bound.
A program may use at most 128 MiB of HBM per device.

v0:
```python
import jax
import jax.numpy as jnp
from jax import lax
from jax.sharding import PartitionSpec as P

BLOCK = 128


def gelu_pull(hidden, upstream):
    pullback = jax.vjp(lambda values: jax.nn.gelu(values, approximate=True), hidden)[1]
    return pullback(upstream)[0]


def per_device(tokens, up_proj, down_proj, keep_mask, cotangent):
    tok_rows, cot_rows = (
        lax.all_gather(tokens, "col", axis=0, tiled=True),
        lax.all_gather(cotangent, "col", axis=0, tiled=True),
    )
    row_blocks, col_blocks = keep_mask.shape
    keep_up = jnp.broadcast_to(
        keep_mask.astype(jnp.bfloat16)[:, None, :, None], (row_blocks, BLOCK, col_blocks, BLOCK)
    )
    keep_up = keep_up.reshape(row_blocks * BLOCK, col_blocks * BLOCK)
    up_masked = up_proj * keep_up
    down_masked = down_proj * keep_up.T
    hidden_part = jnp.dot(tok_rows, up_masked, preferred_element_type=jnp.float32)
    hidden_whole = lax.psum(hidden_part.astype(jnp.bfloat16), "row").astype(jnp.float32)
    active = jax.nn.gelu(hidden_whole, approximate=True).astype(jnp.bfloat16)
    output = lax.psum_scatter(
        jnp.dot(active, down_masked, preferred_element_type=jnp.float32).astype(jnp.bfloat16),
        "col",
        scatter_dimension=0,
        tiled=True,
    )
    upstream_part = jnp.dot(cot_rows, down_masked.T, preferred_element_type=jnp.float32)
    upstream = lax.psum(upstream_part.astype(jnp.bfloat16), "row").astype(jnp.float32)
    hidden_grad = gelu_pull(hidden_whole, upstream).astype(jnp.bfloat16)
    input_grad = lax.psum_scatter(
        jnp.dot(hidden_grad, up_masked.T, preferred_element_type=jnp.float32).astype(jnp.bfloat16),
        "col",
        scatter_dimension=0,
        tiled=True,
    )
    up_sum = jnp.dot(tok_rows.T, hidden_grad, preferred_element_type=jnp.float32)
    down_sum = jnp.dot(active.T, cot_rows, preferred_element_type=jnp.float32)
    up_tile = (up_sum * keep_up.astype(jnp.float32)).astype(jnp.bfloat16)
    down_tile = (down_sum * keep_up.T.astype(jnp.float32)).astype(jnp.bfloat16)
    return (output, input_grad, up_tile, down_tile)


def solution(mesh):
    return jax.shard_map(
        per_device,
        mesh=mesh,
        in_specs=(
            P("col", "row"),
            P("row", "col"),
            P("col", "row"),
            P("row", "col"),
            P("col", "row"),
        ),
        out_specs=(P("col", "row"), P("col", "row"), P("row", "col"), P("col", "row")),
        check_vma=False,
    )
```

profile of v0, /device:TPU:2, one launch (start us, length us, event | category | flops | bytes accessed | tf_op | source)
XLA Modules:
  0.0 430.7 jit_solution(364367606649725258)
XLA Ops:
  7.2 0.0 all-reduce.3.cloned.1.call-start
  7.2 0.7 convert_element_type.45
  7.9 0.0 copy-start
  7.9 41.4 %all_gather.6 = bf16[512,768]{1,0:T(8,128)(2,1)} all-gather(bf16[16,768]{1,0:T(8,128)(2,1)} %param.5), channel_id=1, replica_groups=mesh['row'=16,'col'=32] {'col'}, dimensions={0}, use_global_device_ids=true | all-gather | bytes 811008 | tf_op jit(solution)/shard_map/all_gather | solution.py:16
  49.3 32.1 %all_gather.7 = bf16[512,768]{1,0:T(8,128)(2,1)} all-gather(bf16[16,768]{1,0:T(8,128)(2,1)} %param.9), channel_id=1, replica_groups=mesh['row'=16,'col'=32] {'col'}, dimensions={0}, use_global_device_ids=true | all-gather | bytes 811008 | tf_op jit(solution)/shard_map/all_gather | solution.py:17
  81.4 0.3 broadcast_in_dim.2
  81.7 0.0 copy-done
  81.7 0.2 fusion.18
  81.9 0.6 copy.12
  82.5 0.0 copy-start.1
  82.5 0.0 copy-start.4
  82.5 3.0 fusion.12
  85.5 0.0 copy-done.1
  85.5 0.0 copy-done.4
  85.5 1.7 fusion.13
  87.2 0.0 all-reduce.3.cloned.1.call-update
  87.2 0.0 reduce-scatter.5.cloned.1.call-start
  87.3 116.0 %all-reduce.3.cloned.1.call-done = (bf16[512,768]{0,1:T(8,128)(2,1)}, bf16[512,768]{0,1:T(8,128)(2,1)}) async-done(((bf16[512,768]{0,1:T(8,128)(2,1)}, bf16[512,768]{0,1:T(8,128)(2,1)}), (bf16[512,768]{0,1:T(8,128)(2,1)}, bf16[512,768]{0,1:T(8,128)(2,1)})) %all-reduce.3.cloned.1.call-update) | async-done | bytes 1572880 | tf_op jit(solution)/shard_map/psum | solution.py:27
  203.3 4.1 convolution_convert_fusion
  207.4 0.0 reduce-scatter.5.cloned.1.call-update
  207.4 0.0 copy-start.3
  207.5 0.0 reduce-scatter.3.cloned.1.call-start
  207.5 3.1 convolution_convert_fusion.2
  210.6 0.0 reduce-scatter.3.cloned.1.call-update
  210.7 0.0 copy-done.3
  210.7 3.2 fusion
  213.9 0.0 copy-start.2
  213.9 1.5 copy.14
  215.3 0.0 copy-done.2
  215.3 3.3 multiply_convert_fusion
  218.6 96.4 %reduce-scatter.5.cloned.1.call-done = bf16[16,768]{1,0:T(8,128)(2,1)} async-done(((bf16[512,768]{1,0:T(8,128)(2,1)}), bf16[16,768]{1,0:T(8,128)(2,1)}) %reduce-scatter.5.cloned.1.call-update) | async-done | bytes 24592 | tf_op jit(solution)/shard_map/reduce_scatter | solution.py:38
  315.1 109.1 %reduce-scatter.3.cloned.1.call-done = bf16[16,768]{1,0:T(8,128)(2,1)} async-done(((bf16[512,768]{1,0:T(8,128)(2,1)}), bf16[16,768]{1,0:T(8,128)(2,1)}) %reduce-scatter.3.cloned.1.call-update) | async-done | bytes 24592 | tf_op jit(solution)/shard_map/reduce_scatter | solution.py:29
Async XLA Ops:
  7.2 196.1 %all-reduce.3.cloned.1.call-start = ((), (), s32[]{:S(2)}) async-start(), calls=%async_computation.4 | async-start | bytes 3145728 | tf_op jit(solution)/shard_map/psum | solution.py:27
  7.9 73.8 %copy-start = (bf16[768,768]{1,0:T(8,128)(2,1)S(1)}, bf16[768,768]{1,0:T(8,128)(2,1)}, u32[]{:S(2)}) copy-start(bf16[768,768]{1,0:T(8,128)(2,1)} %param.6) | copy-start | bytes 3538948
  82.5 3.0 copy-start.1
  82.5 3.0 copy-start.4
  87.2 227.8 %reduce-scatter.5.cloned.1.call-start = ((), (), s32[]{:S(2)}) async-start(), calls=%async_computation.3 | async-start | bytes 811008 | tf_op jit(solution)/shard_map/reduce_scatter | solution.py:38
  207.4 3.2 copy-start.3
  207.5 216.7 %reduce-scatter.3.cloned.1.call-start = ((), (), s32[]{:S(2)}) async-start(), calls=%async_computation.2 | async-start | bytes 811008 | tf_op jit(solution)/shard_map/reduce_scatter | solution.py:29
  213.9 1.5 copy-start.2
Sparse Core Ops, SparseCore 0:
  87.4 115.8 all-reduce.2
  207.6 107.4 reduce-scatter.4
  318.7 105.4 reduce-scatter.2
where the time goes:
time: 431 us
  waiting for transfers between devices  322 us (75%)
  blocking collectives  73.5 us (17%)
  matrix products  18.4 us (4%)
  between operations  13.8 us (3%)
    psum x1, waiting for transfers between devices, per_device(): lax.psum(hidden_part.astype(jnp.bfloat16), 'row').astype(jnp.float32)  116 us
    reduce_scatter x1, waiting for transfers between devices, per_device(): lax.psum_scatter(jnp.dot(active, down_masked, preferred_element_type=jnp....  109 us
    reduce_scatter x1, waiting for transfers between devices, per_device(): lax.psum_scatter(jnp.dot(hidden_grad, up_masked.T, preferred_element_type...  96.4 us
    all_gather x1, blocking collectives, per_device(): lax.all_gather(tokens, 'col', axis=0, tiled=True)  41.4 us
    all_gather x1, blocking collectives, per_device(): lax.all_gather(cotangent, 'col', axis=0, tiled=True)  32.1 us
  transfers between devices with their start and end apart: 3, of which 3 were waited for; matrix products, arithmetic and copies ran while one was open for 3% of the time, Pallas kernels for 0%

commit v1 on v0

v1 whole, which is shorter than its diff:
```python
import jax
import jax.numpy as jnp
from jax import lax
from jax.experimental import pallas as pl
from jax.experimental.pallas import tpu as pltpu
from jax.sharding import PartitionSpec as P

MESH = pl.DeviceIdType.MESH
F32 = jnp.float32
BF16 = jnp.bfloat16
B = 128
T = 16
W = 768
NB = W // B
HALF = W // 2
CH = 256
N_CH = W // CH

AG_PER = 18
S1, S2, G1, G2 = 0, 12, 24, 36
R1, R2 = 48, 56
D_UP, D_DN, D_TOK, D_COT, D_ACT, D_HG = 62, 63, 64, 65, 66, 67
N_SEM = 68

GELU_C = 0.7978845608028654
GELU_A = 0.044715


def kernel(tok_ref, up_hbm, down_hbm, mask_ref, cot_ref, out_ref, in_ref, upg_hbm, dng_hbm,
           wup, wdn, ag, part, s1buf, s2buf, acts, pacts, zpart, r1buf, r1sum, r2buf, gbuf,
           ag_send, ag_recv, send, recv, loc):
    row = lax.axis_index("row")
    col = lax.axis_index("col")
    x, y = row % 4, row // 4
    z, k = col // 2, col % 2
    other = 1 - k

    def zdev(d):
        return (row, ((z + d + 16) % 16) * 2 + k)

    def xdev(d):
        return (y * 4 + (x + d) % 4, col)

    def ydev(d):
        return (((y + d) % 4) * 4 + x, col)

    mate = (row, z * 2 + other)

    cp_up = pltpu.make_async_copy(up_hbm, wup.at[k], loc.at[0])
    cp_dn = pltpu.make_async_copy(down_hbm, wdn.at[k], loc.at[1])
    cp_up.start()
    cp_dn.start()

    peers = [zdev(d) for d in (4, -4, 1, -1, 2, -2)] + [xdev(d) for d in (1, 2, 3)] + [ydev(d) for d in (1, 2, 3)] + [mate]
    barrier = pltpu.get_barrier_semaphore()
    for peer in peers:
        pl.semaphore_signal(barrier, inc=1, device_id=peer, device_id_type=MESH)

    def pair_rows(zb):
        zz = (zb + 32) % 16
        return pl.multiple_of((zz % 4) * 64 + ((zz // 4) % 2) * 32, 32)

    def class_rows(zb):
        return pl.multiple_of(((zb + 32) % 4) * 64, 64)

    def block_pos(zb):
        zz = (zb + 32) % 16
        return (zz % 4) * 4 + ((zz // 4) % 2) * 2 + zz // 8

    def block_rows(zb):
        return pl.multiple_of(block_pos(zb) * T, T)

    ag[0, k, pl.ds(block_rows(z), T), :] = tok_ref[...]
    ag[1, k, pl.ds(block_rows(z), T), :] = cot_ref[...]
    cp_up.wait()
    for i in range(NB):
        for j in range(NB):
            m = mask_ref[i, j].astype(F32).astype(BF16)
            wup[k, B * i:B * (i + 1), B * j:B * (j + 1)] = wup[k, B * i:B * (i + 1), B * j:B * (j + 1)] * m
    cp_dn.wait()
    for i in range(NB):
        for j in range(NB):
            m = mask_ref[i, j].astype(F32).astype(BF16)
            wdn[k, B * j:B * (j + 1), B * i:B * (i + 1)] = wdn[k, B * j:B * (j + 1), B * i:B * (i + 1)] * m

    pl.semaphore_wait(barrier, len(peers))

    sends = []

    def push(src, dst, s, r, device):
        copy = pltpu.make_async_remote_copy(src_ref=src, dst_ref=dst, send_sem=s, recv_sem=r, device_id=device, device_id_type=MESH)
        copy.start()
        sends.append(copy)

    def got(dst, s, r):
        pltpu.make_async_remote_copy(src_ref=dst, dst_ref=dst, send_sem=s, recv_sem=r, device_id=mate, device_id_type=MESH).wait_recv()

    def ag_block(a, zb):
        return ag.at[a, k, pl.ds(block_rows(zb), T), :]

    counts = [0, 0]

    def ag_push(a, zb, d):
        n = counts[a]
        counts[a] = n + 1
        push(ag_block(a, zb), ag_block(a, zb), ag_send.at[a * AG_PER + n], ag_recv.at[a * AG_PER + block_pos(zb)], zdev(d))

    def ag_got(a, zb):
        got(ag_block(a, zb), ag_send.at[0], ag_recv.at[a * AG_PER + block_pos(zb)])

    def half_block(a, zb, h):
        return ag.at[a, k, pl.ds(block_rows(zb), T), h * HALF:(h + 1) * HALF]

    for a in range(2):
        for d in (4, -4, 1, -1):
            ag_push(a, z, d)

    push(wup.at[k], wup.at[k], send.at[D_UP], recv.at[D_UP], mate)
    push(wdn.at[k], wdn.at[k], send.at[D_DN], recv.at[D_DN], mate)

    for a in range(2):
        for h, d in ((0, 4), (1, -4)):
            ag_got(a, z - d)
            n = counts[a]
            counts[a] = n + 1
            push(half_block(a, z - d, h), half_block(a, z - d, h), ag_send.at[a * AG_PER + n], ag_recv.at[a * AG_PER + 16 + h], zdev(d))
            for f in (2, -2, 1, -1):
                ag_push(a, z - d, f)
    for a in range(2):
        for h in range(2):
            got(half_block(a, z + 8, h), ag_send.at[0], ag_recv.at[a * AG_PER + 16 + h])
        for f in (1, -1):
            ag_push(a, z + 8, f)

    def ag_rest(a):
        for base in (2, 1, -1):
            for d in (0, 4, -4, 8):
                ag_got(a, z + base + d)
        push(ag.at[a, k], ag.at[a, k], send.at[(D_TOK, D_COT)[a]], recv.at[(D_TOK, D_COT)[a]], mate)

    axes = ((x, xdev, y, ydev), (y, ydev, x, xdev))

    def sem(base, a, h, d):
        i = base + (a * 2 + h) * 3 + d - 1
        return send.at[i], recv.at[i]

    def first_rows(h, d):
        return pl.ds(pl.multiple_of(((axes[h][0] + d) % 4) * 64, 64), 64)

    def second_rows(h, d):
        return pl.ds(pl.multiple_of(axes[h][0] * 64 + ((axes[h][2] + d) % 4) * T, T), T)

    def partial_and_send(a):
        for h in range(2):
            for n in range(N_CH):
                c = slice(n * CH, (n + 1) * CH)
                if a == 0:
                    v = jnp.dot(ag[0, k], wup[h, :, c], preferred_element_type=F32)
                else:
                    v = lax.dot_general(ag[1, k], wdn[h, c, :], (((1,), (1,)), ((), ())), preferred_element_type=F32)
                part[a, h, :, c] = v.astype(BF16)
            for d in (2, 1, 3):
                s, r = sem(S1, a, h, d)
                push(part.at[a, h, first_rows(h, d), :], s1buf.at[a, h, d - 1], s, r, axes[h][1](d))

    def second_stage(a):
        for h in range(2):
            for d in (1, 2, 3):
                got(s1buf.at[a, h, d - 1], *sem(S1, a, h, d))
            total = part[a, h, first_rows(h, 0), :].astype(F32)
            for d in range(3):
                total = total + s1buf[a, h, d].astype(F32)
            part[a, h, first_rows(h, 0), :] = total.astype(BF16)
            for d in (2, 1, 3):
                s, r = sem(S2, a, h, d)
                push(part.at[a, h, second_rows(h, d), :], s2buf.at[a, h, d - 1], s, r, axes[h][3](d))

    def shard(a, h):
        for d in (1, 2, 3):
            got(s2buf.at[a, h, d - 1], *sem(S2, a, h, d))
        total = part[a, h, second_rows(h, 0), :].astype(F32)
        for d in range(3):
            total = total + s2buf[a, h, d].astype(F32)
        return total

    def spread(a, h, value):
        acts[a, h, second_rows(h, 0), :] = value.astype(BF16)
        for d in (2, 1, 3):
            s, r = sem(G1, a, h, d)
            push(acts.at[a, h, second_rows(h, 0), :], acts.at[a, h, second_rows(h, 0), :], s, r, axes[h][3](d))

    def spread_more(a):
        for h in range(2):
            for d in (1, 2, 3):
                got(acts.at[a, h, second_rows(h, -d + 4), :], *sem(G1, a, h, d))
            for d in (2, 1, 3):
                s, r = sem(G2, a, h, d)
                push(acts.at[a, h, first_rows(h, 0), :], acts.at[a, h, first_rows(h, 0), :], s, r, axes[h][1](d))

    def spread_end(a):
        for h in range(2):
            for d in (1, 2, 3):
                got(acts.at[a, h, first_rows(h, -d + 4), :], *sem(G2, a, h, d))

    def z_partial(a):
        for n in range(N_CH):
            c = slice(n * CH, (n + 1) * CH)
            if a == 0:
                v = jnp.dot(acts[0, 0], wdn[0, :, c], preferred_element_type=F32)
                v = v + jnp.dot(acts[0, 1], wdn[1, :, c], preferred_element_type=F32)
            else:
                dims = (((1,), (1,)), ((), ()))
                v = lax.dot_general(acts[1, 0], wup[0, c, :], dims, preferred_element_type=F32)
                v = v + lax.dot_general(acts[1, 1], wup[1, c, :], dims, preferred_element_type=F32)
            zpart[a, :, c] = v.astype(BF16)
        r = R1 + 4 * a
        push(zpart.at[a, pl.ds(pair_rows(z - 2), 32), :], r1buf.at[a, pl.ds(128, 32), :], send.at[r + 2], recv.at[r + 2], zdev(2))
        push(zpart.at[a, pl.ds(pair_rows(z + 2), 32), :], r1buf.at[a, pl.ds(160, 32), :], send.at[r + 3], recv.at[r + 3], zdev(-2))
        push(zpart.at[a, pl.ds(class_rows(z + 1), 64), :], r1buf.at[a, pl.ds(0, 64), :], send.at[r], recv.at[r], zdev(1))
        push(zpart.at[a, pl.ds(class_rows(z - 1), 64), :], r1buf.at[a, pl.ds(64, 64), :], send.at[r + 1], recv.at[r + 1], zdev(-1))
        d = (D_ACT, D_HG)[a]
        push(acts.at[a, other], pacts.at[a], send.at[d], recv.at[d], mate)

    def z_second(a):
        r = R1 + 4 * a
        got(r1buf.at[a, pl.ds(128, 32), :], send.at[r + 2], recv.at[r + 2])
        got(r1buf.at[a, pl.ds(160, 32), :], send.at[r + 3], recv.at[r + 3])
        got(r1buf.at[a, pl.ds(0, 64), :], send.at[r], recv.at[r])
        got(r1buf.at[a, pl.ds(64, 64), :], send.at[r + 1], recv.at[r + 1])
        cls = pl.ds(class_rows(z), 64)
        r1sum[a] = zpart[a, cls, :].astype(F32) + r1buf[a, 0:64, :].astype(F32) + r1buf[a, 64:128, :].astype(F32)
        far = pl.ds(pl.multiple_of(pair_rows(z + 4) - class_rows(z), 32), 32)
        r1sum[a, far, :] = r1sum[a, far, :] + r1buf[a, 128:160, :].astype(F32) + r1buf[a, 160:192, :].astype(F32)
        zpart[a, cls, :] = r1sum[a].astype(BF16)
        q = R2 + 3 * a
        for n, d in enumerate((8, 4, -4)):
            push(zpart.at[a, pl.ds(block_rows(z + d), T), :], r2buf.at[a, n], send.at[q + n], recv.at[q + n], zdev(d))

    def z_end(a, ref):
        q = R2 + 3 * a
        for n in range(3):
            got(r2buf.at[a, n], send.at[q + n], recv.at[q + n])
        mine = pl.ds(pl.multiple_of(block_rows(z) - class_rows(z), T), T)
        total = r1sum[a, mine, :]
        for n in range(3):
            total = total + r2buf[a, n].astype(F32)
        ref[...] = total.astype(BF16)

    def grads(a):
        i = (D_ACT, D_HG)[a]
        got(pacts.at[a], send.at[i], recv.at[i])
        dims = (((0,), (0,)), ((), ()))
        for n in range(N_CH):
            c = slice(n * CH, (n + 1) * CH)
            if a == 0:
                v = lax.dot_general(acts[0, k, :, c], ag[1, k], dims, preferred_element_type=F32)
                v = v + lax.dot_general(pacts[0, :, c], ag[1, other], dims, preferred_element_type=F32)
            else:
                v = lax.dot_general(ag[0, k, :, c], acts[1, k], dims, preferred_element_type=F32)
                v = v + lax.dot_general(ag[0, other, :, c], pacts[1], dims, preferred_element_type=F32)
            for i in range(CH // B):
                for j in range(NB):
                    p = n * (CH // B) + i
                    m = (mask_ref[j, p] if a == 0 else mask_ref[p, j]).astype(F32)
                    gbuf[a, B * p:B * (p + 1), B * j:B * (j + 1)] = (v[B * i:B * (i + 1), B * j:B * (j + 1)] * m).astype(BF16)

    ag_rest(0)
    got(wup.at[other], send.at[D_UP], recv.at[D_UP])
    partial_and_send(0)
    second_stage(0)
    ag_rest(1)
    got(wdn.at[other], send.at[D_DN], recv.at[D_DN])
    partial_and_send(1)
    pre = []
    for h in range(2):
        v = shard(0, h)
        t = jnp.tanh(GELU_C * (v + GELU_A * v * v * v))
        spread(0, h, 0.5 * v * (1.0 + t))
        pre.append(0.5 * (1.0 + t) + 0.5 * v * (1.0 - t * t) * (GELU_C * (1.0 + 3.0 * GELU_A * v * v)))
    spread_more(0)
    second_stage(1)
    for h in range(2):
        spread(1, h, pre[h] * shard(1, h))
    spread_end(0)
    z_partial(0)
    spread_more(1)
    got(ag.at[0, other], send.at[D_TOK], recv.at[D_TOK])
    got(ag.at[1, other], send.at[D_COT], recv.at[D_COT])
    z_second(0)
    spread_end(1)
    z_partial(1)
    grads(0)
    cp_dg = pltpu.make_async_copy(gbuf.at[0], dng_hbm, loc.at[0])
    cp_dg.start()
    z_second(1)
    grads(1)
    cp_ug = pltpu.make_async_copy(gbuf.at[1], upg_hbm, loc.at[1])
    cp_ug.start()
    z_end(0, out_ref)
    z_end(1, in_ref)
    cp_dg.wait()
    cp_ug.wait()
    for copy in sends:
        copy.wait_send()


def per_device(tokens, up_proj, down_proj, keep_mask, cotangent):
    vmem = pl.BlockSpec(memory_space=pltpu.VMEM)
    hbm = pl.BlockSpec(memory_space=pl.ANY)
    smem = pl.BlockSpec(memory_space=pltpu.SMEM)
    small = jax.ShapeDtypeStruct((T, W), BF16)
    big = jax.ShapeDtypeStruct((W, W), BF16)
    return pl.pallas_call(
        kernel,
        out_shape=(small, small, big, big),
        in_specs=[vmem, hbm, hbm, smem, vmem],
        out_specs=(vmem, vmem, hbm, hbm),
        scratch_shapes=[
            pltpu.VMEM((2, W, W), BF16),
            pltpu.VMEM((2, W, W), BF16),
            pltpu.VMEM((2, 2, 256, W), BF16),
            pltpu.VMEM((2, 2, 256, W), BF16),
            pltpu.VMEM((2, 2, 3, 64, W), BF16),
            pltpu.VMEM((2, 2, 3, T, W), BF16),
            pltpu.VMEM((2, 2, 256, W), BF16),
            pltpu.VMEM((2, 256, W), BF16),
            pltpu.VMEM((2, 256, W), BF16),
            pltpu.VMEM((2, 192, W), BF16),
            pltpu.VMEM((2, 64, W), F32),
            pltpu.VMEM((2, 3, T, W), BF16),
            pltpu.VMEM((2, W, W), BF16),
            pltpu.SemaphoreType.DMA((2 * AG_PER,)),
            pltpu.SemaphoreType.DMA((2 * AG_PER,)),
            pltpu.SemaphoreType.DMA((N_SEM,)),
            pltpu.SemaphoreType.DMA((N_SEM,)),
            pltpu.SemaphoreType.DMA((2,)),
        ],
        compiler_params=pltpu.CompilerParams(collective_id=0, has_side_effects=True, vmem_limit_bytes=40 * 2**20),
        cost_estimate=pl.CostEstimate(flops=3_700_000_000, bytes_accessed=5_000_000, transcendentals=30000),
        name="ffn",
    )(tokens, up_proj, down_proj, keep_mask, cotangent)


def solution(mesh):
    return jax.shard_map(
        per_device,
        mesh=mesh,
        in_specs=(P("col", "row"), P("row", "col"), P("col", "row"), P("row", "col"), P("col", "row")),
        out_specs=(P("col", "row"), P("col", "row"), P("row", "col"), P("col", "row")),
        check_vma=False,
    )
```

time: 431 us -> 92.1 us (0.21)
  the two profiles are of different devices: /device:TPU:2 before, /device:TPU:32 now
where the time goes in v1:
time: 92.1 us; the launch traced here: 91.7 us
  Pallas kernels  83.1 us (90%)
  local copies, waits for them, and re-layouts  7.94 us (9%)
    pallas_call x1, Pallas kernels, per_device(): pl.pallas_call(kernel, out_shape=(small, small, big, big), in_specs=[vmem...  83.1 us
    unnamed x14, local copies, waits for them, and re-layouts  7.94 us

profile of v1, /device:TPU:32, one launch (start us, length us, event | category | flops | bytes accessed | tf_op | source)
XLA Modules:
  0.0 91.7 jit_solution(6802073371915746908)
XLA Ops:
  0.6 0.0 copy-start
  0.6 1.3 %copy-done = bf16[768,768]{1,0:T(8,128)(2,1)S(1)} copy-done((bf16[768,768]{1,0:T(8,128)(2,1)S(1)}, bf16[768,768]{1,0:T(8,128)(2,1)}, u32[]{:S(2)}) %copy-start) | copy-done | bytes 1179672
  1.9 0.0 copy-start.1
  1.9 1.3 %copy-done.1 = bf16[768,768]{1,0:T(8,128)(2,1)S(1)} copy-done((bf16[768,768]{1,0:T(8,128)(2,1)S(1)}, bf16[768,768]{1,0:T(8,128)(2,1)}, u32[]{:S(2)}) %copy-start.1) | copy-done | bytes 1179672
  3.2 0.0 copy-start.2
  3.2 0.7 copy-done.2
  3.9 0.0 copy-start.3
  3.9 0.7 copy-done.3
  4.7 0.0 copy-start.4
  4.7 0.7 copy-done.4
  5.3 83.1 %ffn.1 = (bf16[16,768]{1,0:T(8,128)(2,1)S(1)}, bf16[16,768]{1,0:T(8,128)(2,1)S(1)}, bf16[768,768]{1,0:T(8,128)(2,1)S(1)}, bf16[768,768]{1,0:T(8,128)(2,1)S(1)}) custom-call(bf16[16,768]{1,0:T(8,128)(2,1)S(1)} %copy-done.2, bf16[768,768]{1,0:T(8,128)(2,1)S(1)} %copy-done, bf16[768,768]{1,0:T(8,128)(2,1)S(1)} %copy-done.1, s32[6,6]{1,0:T(8,128)S(1)} %copy-done.4, ...), custom_call_target="tpu_custom_call" | custom-call | flops 3700000000 | bytes 5000000 | tf_op jit(solution)/shard_map/ffn/pallas_call | solution.py:313
  88.5 0.6 copy.13
  89.1 0.6 copy.14
  89.7 1.0 %copy.15 = bf16[768,768]{1,0:T(8,128)(2,1)} copy(bf16[768,768]{1,0:T(8,128)(2,1)S(1)} %get-tuple-element.10) | data formatting | bytes 2359296
  90.7 1.0 %copy.16 = bf16[768,768]{1,0:T(8,128)(2,1)} copy(bf16[768,768]{1,0:T(8,128)(2,1)S(1)} %get-tuple-element.11) | data formatting | bytes 2359296
Async XLA Ops:
  0.6 1.3 %copy-start = (bf16[768,768]{1,0:T(8,128)(2,1)S(1)}, bf16[768,768]{1,0:T(8,128)(2,1)}, u32[]{:S(2)}) copy-start(bf16[768,768]{1,0:T(8,128)(2,1)} %up_hbm.1) | copy-start | bytes 3538948
  1.9 1.3 %copy-start.1 = (bf16[768,768]{1,0:T(8,128)(2,1)S(1)}, bf16[768,768]{1,0:T(8,128)(2,1)}, u32[]{:S(2)}) copy-start(bf16[768,768]{1,0:T(8,128)(2,1)} %down_hbm.1) | copy-start | bytes 3538948
  3.2 0.7 copy-start.2
  3.9 0.7 copy-start.3
  4.7 0.7 copy-start.4

commit v2 on v1

--- a/solution.py
+++ b/solution.py
@@ -26,9 +26,9 @@
 GELU_A = 0.044715
 
 
-def kernel(tok_ref, up_hbm, down_hbm, mask_ref, cot_ref, out_ref, in_ref, upg_hbm, dng_hbm,
-           wup, wdn, ag, part, s1buf, s2buf, acts, pacts, zpart, r1buf, r1sum, r2buf, gbuf,
-           ag_send, ag_recv, send, recv, loc):
+def kernel(tok_hbm, up_hbm, down_hbm, mask_hbm, cot_hbm, out_hbm, in_hbm, upg_hbm, dng_hbm,
+           wup, wdn, ag, part, s1buf, s2buf, acts, pacts, zpart, r1buf, r1sum, r2buf, gbuf, obuf, mask_ref,
+           ag_send, ag_recv, send, recv, loc, mate_sem):
     row = lax.axis_index("row")
     col = lax.axis_index("col")
     x, y = row % 4, row // 4
@@ -46,32 +46,76 @@
 
     mate = (row, z * 2 + other)
 
-    cp_up = pltpu.make_async_copy(up_hbm, wup.at[k], loc.at[0])
-    cp_dn = pltpu.make_async_copy(down_hbm, wdn.at[k], loc.at[1])
-    cp_up.start()
-    cp_dn.start()
-
-    peers = [zdev(d) for d in (4, -4, 1, -1, 2, -2)] + [xdev(d) for d in (1, 2, 3)] + [ydev(d) for d in (1, 2, 3)] + [mate]
+    def pair_rows(zb):
+        zz = (zb + 32) % 16
+        return pl.multiple_of((zz % 4) * 64 + ((zz // 4) % 2) * 32, 32)
+
+    def class_rows(zb):
+        return pl.multiple_of(((zb + 32) % 4) * 64, 64)
+
+    def block_pos(zb):
+        zz = (zb + 32) % 16
+        return (zz % 4) * 4 + ((zz // 4) % 2) * 2 + zz // 8
+
+    def block_rows(zb):
+        return pl.multiple_of(block_pos(zb) * T, T)
+
+    mine = pl.ds(block_rows(z), T)
+    cp_tok = pltpu.make_async_copy(tok_hbm, ag.at[0, k, mine, :], loc.at[0])
+    cp_cot = pltpu.make_async_copy(cot_hbm, ag.at[1, k, mine, :], loc.at[1])
+    cp_mask = pltpu.make_async_copy(mask_hbm, mask_ref, loc.at[2])
+    cp_up = pltpu.make_async_copy(up_hbm, wup.at[k], loc.at[3])
+    cp_dn = pltpu.make_async_copy(down_hbm, wdn.at[k], loc.at[4])
+    for cp in (cp_tok, cp_cot, cp_mask, cp_up, cp_dn):
+        cp.start()
+
+    peers = [zdev(d) for d in (4, -4, 1, -1, 2, -2)] + [xdev(d) for d in (1, 2, 3)] + [ydev(d) for d in (1, 2, 3)]
     barrier = pltpu.get_barrier_semaphore()
     for peer in peers:
         pl.semaphore_signal(barrier, inc=1, device_id=peer, device_id_type=MESH)
 
-    def pair_rows(zb):
-        zz = (zb + 32) % 16
-        return pl.multiple_of((zz % 4) * 64 + ((zz // 4) % 2) * 32, 32)
-
-    def class_rows(zb):
-        return pl.multiple_of(((zb + 32) % 4) * 64, 64)
-
-    def block_pos(zb):
-        zz = (zb + 32) % 16
-        return (zz % 4) * 4 + ((zz // 4) % 2) * 2 + zz // 8
-
-    def block_rows(zb):
-        return pl.multiple_of(block_pos(zb) * T, T)
-
-    ag[0, k, pl.ds(block_rows(z), T), :] = tok_ref[...]
-    ag[1, k, pl.ds(block_rows(z), T), :] = cot_ref[...]
+    @pl.when(k == 0)
+    def _():
+        pl.semaphore_signal(barrier, inc=1, device_id=mate, device_id_type=MESH)
+
+    cp_tok.wait()
+    cp_cot.wait()
+    pl.semaphore_wait(barrier, len(peers) + k)
+
+    sends = []
+
+    def push(src, dst, s, r, device):
+        copy = pltpu.make_async_remote_copy(src_ref=src, dst_ref=dst, send_sem=s, recv_sem=r, device_id=device, device_id_type=MESH)
+        copy.start()
+        sends.append(copy)
+
+    def got(dst, s, r):
+        pltpu.make_async_remote_copy(src_ref=dst, dst_ref=dst, send_sem=s, recv_sem=r, device_id=mate, device_id_type=MESH).wait_recv()
+
+    def ag_block(a, zb):
+        return ag.at[a, k, pl.ds(block_rows(zb), T), :]
+
+    counts = [0, 0]
+
+    def ag_push(a, zb, d):
+        n = counts[a]
+        counts[a] = n + 1
+        push(ag_block(a, zb), ag_block(a, zb), ag_send.at[a * AG_PER + n], ag_recv.at[a * AG_PER + block_pos(zb)], zdev(d))
+
+    def ag_got(a, zb):
+        got(ag_block(a, zb), ag_send.at[0], ag_recv.at[a * AG_PER + block_pos(zb)])
+
+    def half_block(a, zb, h):
+        return ag.at[a, k, pl.ds(block_rows(zb), T), h * HALF:(h + 1) * HALF]
+
+    for d in (4, -4, 1, -1):
+        ag_push(0, z, d)
+
+    @pl.when(k == 1)
+    def _():
+        pl.semaphore_signal(mate_sem, inc=1, device_id=mate, device_id_type=MESH)
+
+    cp_mask.wait()
     cp_up.wait()
     for i in range(NB):
         for j in range(NB):
@@ -83,59 +127,29 @@
             m = mask_ref[i, j].astype(F32).astype(BF16)
             wdn[k, B * j:B * (j + 1), B * i:B * (i + 1)] = wdn[k, B * j:B * (j + 1), B * i:B * (i + 1)] * m
 
-    pl.semaphore_wait(barrier, len(peers))
-
-    sends = []
-
-    def push(src, dst, s, r, device):
-        copy = pltpu.make_async_remote_copy(src_ref=src, dst_ref=dst, send_sem=s, recv_sem=r, device_id=device, device_id_type=MESH)
-        copy.start()
-        sends.append(copy)
-
-    def got(dst, s, r):
-        pltpu.make_async_remote_copy(src_ref=dst, dst_ref=dst, send_sem=s, recv_sem=r, device_id=mate, device_id_type=MESH).wait_recv()
-
-    def ag_block(a, zb):
-        return ag.at[a, k, pl.ds(block_rows(zb), T), :]
-
-    counts = [0, 0]
-
-    def ag_push(a, zb, d):
-        n = counts[a]
-        counts[a] = n + 1
-        push(ag_block(a, zb), ag_block(a, zb), ag_send.at[a * AG_PER + n], ag_recv.at[a * AG_PER + block_pos(zb)], zdev(d))
-
-    def ag_got(a, zb):
-        got(ag_block(a, zb), ag_send.at[0], ag_recv.at[a * AG_PER + block_pos(zb)])
-
-    def half_block(a, zb, h):
-        return ag.at[a, k, pl.ds(block_rows(zb), T), h * HALF:(h + 1) * HALF]
-
-    for a in range(2):
-        for d in (4, -4, 1, -1):
-            ag_push(a, z, d)
-
-    push(wup.at[k], wup.at[k], send.at[D_UP], recv.at[D_UP], mate)
-    push(wdn.at[k], wdn.at[k], send.at[D_DN], recv.at[D_DN], mate)
-
-    for a in range(2):
+    def ag_forward(a):
         for h, d in ((0, 4), (1, -4)):
             ag_got(a, z - d)
             n = counts[a]
             counts[a] = n + 1
             push(half_block(a, z - d, h), half_block(a, z - d, h), ag_send.at[a * AG_PER + n], ag_recv.at[a * AG_PER + 16 + h], zdev(d))
-            for f in (2, -2, 1, -1):
+            for f in (1, -1):
                 ag_push(a, z - d, f)
-    for a in range(2):
+
+    def ag_relay(a, dist):
+        for f in (1, -1):
+            ag_got(a, z - f * dist)
+            ag_push(a, z - f * dist, f)
+
+    def ag_opposite(a):
         for h in range(2):
             got(half_block(a, z + 8, h), ag_send.at[0], ag_recv.at[a * AG_PER + 16 + h])
         for f in (1, -1):
             ag_push(a, z + 8, f)
 
     def ag_rest(a):
-        for base in (2, 1, -1):
-            for d in (0, 4, -4, 8):
-                ag_got(a, z + base + d)
+        for d in (-3, 3, -7, 7, 2, -2, 6, -6):
+            ag_got(a, z + d)
         push(ag.at[a, k], ag.at[a, k], send.at[(D_TOK, D_COT)[a]], recv.at[(D_TOK, D_COT)[a]], mate)
 
     axes = ((x, xdev, y, ydev), (y, ydev, x, xdev))
@@ -236,15 +250,14 @@
         for n, d in enumerate((8, 4, -4)):
             push(zpart.at[a, pl.ds(block_rows(z + d), T), :], r2buf.at[a, n], send.at[q + n], recv.at[q + n], zdev(d))
 
-    def z_end(a, ref):
+    def z_end(a):
         q = R2 + 3 * a
         for n in range(3):
             got(r2buf.at[a, n], send.at[q + n], recv.at[q + n])
-        mine = pl.ds(pl.multiple_of(block_rows(z) - class_rows(z), T), T)
-        total = r1sum[a, mine, :]
+        total = r1sum[a, pl.ds(pl.multiple_of(block_rows(z) - class_rows(z), T), T), :]
         for n in range(3):
             total = total + r2buf[a, n].astype(F32)
-        ref[...] = total.astype(BF16)
+        obuf[a] = total.astype(BF16)
 
     def grads(a):
         i = (D_ACT, D_HG)[a]
@@ -264,9 +277,26 @@
                     m = (mask_ref[j, p] if a == 0 else mask_ref[p, j]).astype(F32)
                     gbuf[a, B * p:B * (p + 1), B * j:B * (j + 1)] = (v[B * i:B * (i + 1), B * j:B * (j + 1)] * m).astype(BF16)
 
+    ag_forward(0)
+    ag_relay(0, 1)
+    for d in (4, -4, 1, -1):
+        ag_push(1, z, d)
+
+    @pl.when(k == 0)
+    def _():
+        pl.semaphore_wait(mate_sem, 1)
+
+    push(wup.at[k], wup.at[k], send.at[D_UP], recv.at[D_UP], mate)
+    push(wdn.at[k], wdn.at[k], send.at[D_DN], recv.at[D_DN], mate)
+    ag_relay(0, 5)
+    ag_opposite(0)
+    ag_forward(1)
+    ag_relay(1, 1)
     ag_rest(0)
     got(wup.at[other], send.at[D_UP], recv.at[D_UP])
     partial_and_send(0)
+    ag_relay(1, 5)
+    ag_opposite(1)
     second_stage(0)
     ag_rest(1)
     got(wdn.at[other], send.at[D_DN], recv.at[D_DN])
@@ -296,25 +326,45 @@
     grads(1)
     cp_ug = pltpu.make_async_copy(gbuf.at[1], upg_hbm, loc.at[1])
     cp_ug.start()
-    z_end(0, out_ref)
-    z_end(1, in_ref)
-    cp_dg.wait()
-    cp_ug.wait()
+    z_end(0)
+    cp_out = pltpu.make_async_copy(obuf.at[0], out_hbm, loc.at[2])
+    cp_out.start()
+    z_end(1)
+    cp_in = pltpu.make_async_copy(obuf.at[1], in_hbm, loc.at[3])
+    cp_in.start()
+    for cp in (cp_dg, cp_ug, cp_out, cp_in):
+        cp.wait()
     for copy in sends:
         copy.wait_send()
 
 
+def move_out(*refs):
+    given, taken, held, sems = refs[:4], refs[4:8], refs[8:12], refs[12]
+    copies = []
+    for g, t, h in zip(given, taken, held):
+        rows = min(h.shape[0], 256)
+        for r in range(0, h.shape[0], rows):
+            copies.append([p.at[pl.ds(r, rows), :] for p in (g, h, t)])
+    loads = [pltpu.make_async_copy(g, h, sems.at[0, n]) for n, (g, h, t) in enumerate(copies)]
+    stores = [pltpu.make_async_copy(h, t, sems.at[1, n]) for n, (g, h, t) in enumerate(copies)]
+    for load in loads:
+        load.start()
+    for load, store in zip(loads, stores):
+        load.wait()
+        store.start()
+    for store in stores:
+        store.wait()
+
+
 def per_device(tokens, up_proj, down_proj, keep_mask, cotangent):
-    vmem = pl.BlockSpec(memory_space=pltpu.VMEM)
     hbm = pl.BlockSpec(memory_space=pl.ANY)
-    smem = pl.BlockSpec(memory_space=pltpu.SMEM)
     small = jax.ShapeDtypeStruct((T, W), BF16)
     big = jax.ShapeDtypeStruct((W, W), BF16)
-    return pl.pallas_call(
+    results = pl.pallas_call(
         kernel,
         out_shape=(small, small, big, big),
-        in_specs=[vmem, hbm, hbm, smem, vmem],
-        out_specs=(vmem, vmem, hbm, hbm),
+        in_specs=[pl.BlockSpec(memory_space=pltpu.HBM)] * 5,
+        out_specs=(hbm,) * 4,
         scratch_shapes=[
             pltpu.VMEM((2, W, W), BF16),
             pltpu.VMEM((2, W, W), BF16),
@@ -329,16 +379,28 @@
             pltpu.VMEM((2, 64, W), F32),
             pltpu.VMEM((2, 3, T, W), BF16),
             pltpu.VMEM((2, W, W), BF16),
+            pltpu.VMEM((2, T, W), BF16),
+            pltpu.SMEM((NB, NB), jnp.int32),
             pltpu.SemaphoreType.DMA((2 * AG_PER,)),
             pltpu.SemaphoreType.DMA((2 * AG_PER,)),
             pltpu.SemaphoreType.DMA((N_SEM,)),
             pltpu.SemaphoreType.DMA((N_SEM,)),
-            pltpu.SemaphoreType.DMA((2,)),
+            pltpu.SemaphoreType.DMA((5,)),
+            pltpu.SemaphoreType.REGULAR,
         ],
-        compiler_params=pltpu.CompilerParams(collective_id=0, has_side_effects=True, vmem_limit_bytes=40 * 2**20),
+        compiler_params=pltpu.CompilerParams(collective_id=0, has_side_effects=True, vmem_limit_bytes=60 * 2**20),
         cost_estimate=pl.CostEstimate(flops=3_700_000_000, bytes_accessed=5_000_000, transcendentals=30000),
         name="ffn",
     )(tokens, up_proj, down_proj, keep_mask, cotangent)
+    return pl.pallas_call(
+        move_out,
+        out_shape=(small, small, big, big),
+        in_specs=[hbm] * 4,
+        out_specs=(hbm,) * 4,
+        scratch_shapes=[pltpu.VMEM(r.shape, BF16) for r in (small, small, big, big)] + [pltpu.SemaphoreType.DMA((2, 8))],
+        compiler_params=pltpu.CompilerParams(vmem_limit_bytes=60 * 2**20),
+        name="move_out",
+    )(*results)
 
 
 def solution(mesh):

time: 92.1 us -> 82.6 us (0.90)
  the two profiles are of different devices: /device:TPU:32 before, /device:TPU:2 now
where the time goes in v2:
time: 82.6 us; the launch traced here: 82.4 us
  Pallas kernels  81.8 us (99%)
    pallas_call x1, Pallas kernels, per_device(): pl.pallas_call(kernel, out_shape=(small, small, big, big), in_specs=[pl.B...  79.2 us
    pallas_call x1, Pallas kernels, per_device(): pl.pallas_call(move_out, out_shape=(small, small, big, big), in_specs=[hb...  2.56 us

profile of v2, /device:TPU:2, one launch (start us, length us, event | category | flops | bytes accessed | tf_op | source)
XLA Modules:
  0.0 82.4 jit_solution(779493947777248776)
XLA Ops:
  0.6 79.2 %ffn.1 = (bf16[16,768]{1,0:T(8,128)(2,1)}, bf16[16,768]{1,0:T(8,128)(2,1)}, bf16[768,768]{1,0:T(8,128)(2,1)}, bf16[768,768]{1,0:T(8,128)(2,1)}) custom-call(bf16[16,768]{1,0:T(8,128)(2,1)} %tok_hbm.1, bf16[768,768]{1,0:T(8,128)(2,1)} %up_hbm.1, bf16[768,768]{1,0:T(8,128)(2,1)} %down_hbm.1, s32[6,6]{1,0:T(8,128)} %mask_hbm.1, bf16[16,768]{1,0:T(8,128)(2,1)} %cot_hbm.1), custom_call_target="tpu_custom_call" | custom-call | flops 3700000000 | bytes 5000000 | tf_op jit(solution)/shard_map/ffn/pallas_call | solution.py:363
  79.8 2.6 %move_out.1 = (bf16[16,768]{1,0:T(8,128)(2,1)}, bf16[16,768]{1,0:T(8,128)(2,1)}, bf16[768,768]{1,0:T(8,128)(2,1)}, bf16[768,768]{1,0:T(8,128)(2,1)}) custom-call(bf16[16,768]{1,0:T(8,128)(2,1)} %get-tuple-element.8.refs_0_, bf16[16,768]{1,0:T(8,128)(2,1)} %get-tuple-element.9.refs_1_, bf16[768,768]{1,0:T(8,128)(2,1)} %get-tuple-element.10.refs_2_, ...), custom_call_target="tpu_custom_call" | custom-call | tf_op jit(solution)/shard_map/move_out/pallas_call | solution.py:395

commit v3 on v2

--- a/solution.py
+++ b/solution.py
@@ -307,13 +307,13 @@
         t = jnp.tanh(GELU_C * (v + GELU_A * v * v * v))
         spread(0, h, 0.5 * v * (1.0 + t))
         pre.append(0.5 * (1.0 + t) + 0.5 * v * (1.0 - t * t) * (GELU_C * (1.0 + 3.0 * GELU_A * v * v)))
+    second_stage(1)
     spread_more(0)
-    second_stage(1)
     for h in range(2):
         spread(1, h, pre[h] * shard(1, h))
+    spread_more(1)
     spread_end(0)
     z_partial(0)
-    spread_more(1)
     got(ag.at[0, other], send.at[D_TOK], recv.at[D_TOK])
     got(ag.at[1, other], send.at[D_COT], recv.at[D_COT])
     z_second(0)

time: 82.6 us -> 81.2 us (0.983)
  Pallas kernels: 81.8 us -> 80.4 us
    pallas_call x1, Pallas kernels: 79.2 us -> 77.8 us  [per_device(): pl.pallas_call(kernel, out_shape=(small, small, big, big), in_specs=[pl.B...]
where the time goes in v3:
time: 81.2 us; the launch traced here: 81 us
  Pallas kernels  80.4 us (99%)
    pallas_call x1, Pallas kernels, per_device(): pl.pallas_call(kernel, out_shape=(small, small, big, big), in_specs=[pl.B...  77.8 us
    pallas_call x1, Pallas kernels, per_device(): pl.pallas_call(move_out, out_shape=(small, small, big, big), in_specs=[hb...  2.56 us

profile of v3, /device:TPU:2, one launch (start us, length us, event | category | flops | bytes accessed | tf_op | source)
XLA Modules:
  0.0 81.0 jit_solution(10885996299170901624)
XLA Ops:
  0.6 77.8 %ffn.1 = (bf16[16,768]{1,0:T(8,128)(2,1)}, bf16[16,768]{1,0:T(8,128)(2,1)}, bf16[768,768]{1,0:T(8,128)(2,1)}, bf16[768,768]{1,0:T(8,128)(2,1)}) custom-call(bf16[16,768]{1,0:T(8,128)(2,1)} %tok_hbm.1, bf16[768,768]{1,0:T(8,128)(2,1)} %up_hbm.1, bf16[768,768]{1,0:T(8,128)(2,1)} %down_hbm.1, s32[6,6]{1,0:T(8,128)} %mask_hbm.1, bf16[16,768]{1,0:T(8,128)(2,1)} %cot_hbm.1), custom_call_target="tpu_custom_call" | custom-call | flops 3700000000 | bytes 5000000 | tf_op jit(solution)/shard_map/ffn/pallas_call | solution.py:363
  78.5 2.6 %move_out.1 = (bf16[16,768]{1,0:T(8,128)(2,1)}, bf16[16,768]{1,0:T(8,128)(2,1)}, bf16[768,768]{1,0:T(8,128)(2,1)}, bf16[768,768]{1,0:T(8,128)(2,1)}) custom-call(bf16[16,768]{1,0:T(8,128)(2,1)} %get-tuple-element.8.refs_0_, bf16[16,768]{1,0:T(8,128)(2,1)} %get-tuple-element.9.refs_1_, bf16[768,768]{1,0:T(8,128)(2,1)} %get-tuple-element.10.refs_2_, ...), custom_call_target="tpu_custom_call" | custom-call | tf_op jit(solution)/shard_map/move_out/pallas_call | solution.py:395

commit v4 on v3

--- a/solution.py
+++ b/solution.py
@@ -314,11 +314,11 @@
     spread_more(1)
     spread_end(0)
     z_partial(0)
+    spread_end(1)
+    z_partial(1)
+    z_second(0)
     got(ag.at[0, other], send.at[D_TOK], recv.at[D_TOK])
     got(ag.at[1, other], send.at[D_COT], recv.at[D_COT])
-    z_second(0)
-    spread_end(1)
-    z_partial(1)
     grads(0)
     cp_dg = pltpu.make_async_copy(gbuf.at[0], dng_hbm, loc.at[0])
     cp_dg.start()

time: 81.2 us -> 79.2 us (0.975)
  Pallas kernels: 80.4 us -> 78.4 us
    pallas_call x1, Pallas kernels: 77.8 us -> 75.9 us  [per_device(): pl.pallas_call(kernel, out_shape=(small, small, big, big), in_specs=[pl.B...]
where the time goes in v4:
time: 79.2 us; the launch traced here: 79.1 us
  Pallas kernels  78.4 us (99%)
    pallas_call x1, Pallas kernels, per_device(): pl.pallas_call(kernel, out_shape=(small, small, big, big), in_specs=[pl.B...  75.9 us
    pallas_call x1, Pallas kernels, per_device(): pl.pallas_call(move_out, out_shape=(small, small, big, big), in_specs=[hb...  2.56 us

profile of v4, /device:TPU:2, one launch (start us, length us, event | category | flops | bytes accessed | tf_op | source)
XLA Modules:
  0.0 79.1 jit_solution(3429370682219378901)
XLA Ops:
  0.6 75.9 %ffn.1 = (bf16[16,768]{1,0:T(8,128)(2,1)}, bf16[16,768]{1,0:T(8,128)(2,1)}, bf16[768,768]{1,0:T(8,128)(2,1)}, bf16[768,768]{1,0:T(8,128)(2,1)}) custom-call(bf16[16,768]{1,0:T(8,128)(2,1)} %tok_hbm.1, bf16[768,768]{1,0:T(8,128)(2,1)} %up_hbm.1, bf16[768,768]{1,0:T(8,128)(2,1)} %down_hbm.1, s32[6,6]{1,0:T(8,128)} %mask_hbm.1, bf16[16,768]{1,0:T(8,128)(2,1)} %cot_hbm.1), custom_call_target="tpu_custom_call" | custom-call | flops 3700000000 | bytes 5000000 | tf_op jit(solution)/shard_map/ffn/pallas_call | solution.py:363
  76.5 2.6 %move_out.1 = (bf16[16,768]{1,0:T(8,128)(2,1)}, bf16[16,768]{1,0:T(8,128)(2,1)}, bf16[768,768]{1,0:T(8,128)(2,1)}, bf16[768,768]{1,0:T(8,128)(2,1)}) custom-call(bf16[16,768]{1,0:T(8,128)(2,1)} %get-tuple-element.8.refs_0_, bf16[16,768]{1,0:T(8,128)(2,1)} %get-tuple-element.9.refs_1_, bf16[768,768]{1,0:T(8,128)(2,1)} %get-tuple-element.10.refs_2_, ...), custom_call_target="tpu_custom_call" | custom-call | tf_op jit(solution)/shard_map/move_out/pallas_call | solution.py:395

commit v5 on v4

--- a/solution.py
+++ b/solution.py
@@ -317,12 +317,12 @@
     spread_end(1)
     z_partial(1)
     z_second(0)
+    z_second(1)
     got(ag.at[0, other], send.at[D_TOK], recv.at[D_TOK])
     got(ag.at[1, other], send.at[D_COT], recv.at[D_COT])
     grads(0)
     cp_dg = pltpu.make_async_copy(gbuf.at[0], dng_hbm, loc.at[0])
     cp_dg.start()
-    z_second(1)
     grads(1)
     cp_ug = pltpu.make_async_copy(gbuf.at[1], upg_hbm, loc.at[1])
     cp_ug.start()

time: 79.2 us -> 79.4 us (level)
  no operation moved by 1% of the time
where the time goes in v5:
time: 79.4 us; the launch traced here: 79.3 us
  Pallas kernels  78.6 us (99%)
    pallas_call x1, Pallas kernels, per_device(): pl.pallas_call(kernel, out_shape=(small, small, big, big), in_specs=[pl.B...  76.1 us
    pallas_call x1, Pallas kernels, per_device(): pl.pallas_call(move_out, out_shape=(small, small, big, big), in_specs=[hb...  2.56 us

profile of v5, /device:TPU:2, one launch (start us, length us, event | category | flops | bytes accessed | tf_op | source)
XLA Modules:
  0.0 79.3 jit_solution(11406276565268540308)
XLA Ops:
  0.6 76.1 %ffn.1 = (bf16[16,768]{1,0:T(8,128)(2,1)}, bf16[16,768]{1,0:T(8,128)(2,1)}, bf16[768,768]{1,0:T(8,128)(2,1)}, bf16[768,768]{1,0:T(8,128)(2,1)}) custom-call(bf16[16,768]{1,0:T(8,128)(2,1)} %tok_hbm.1, bf16[768,768]{1,0:T(8,128)(2,1)} %up_hbm.1, bf16[768,768]{1,0:T(8,128)(2,1)} %down_hbm.1, s32[6,6]{1,0:T(8,128)} %mask_hbm.1, bf16[16,768]{1,0:T(8,128)(2,1)} %cot_hbm.1), custom_call_target="tpu_custom_call" | custom-call | flops 3700000000 | bytes 5000000 | tf_op jit(solution)/shard_map/ffn/pallas_call | solution.py:363
  76.7 2.6 %move_out.1 = (bf16[16,768]{1,0:T(8,128)(2,1)}, bf16[16,768]{1,0:T(8,128)(2,1)}, bf16[768,768]{1,0:T(8,128)(2,1)}, bf16[768,768]{1,0:T(8,128)(2,1)}) custom-call(bf16[16,768]{1,0:T(8,128)(2,1)} %get-tuple-element.8.refs_0_, bf16[16,768]{1,0:T(8,128)(2,1)} %get-tuple-element.9.refs_1_, bf16[768,768]{1,0:T(8,128)(2,1)} %get-tuple-element.10.refs_2_, ...), custom_call_target="tpu_custom_call" | custom-call | tf_op jit(solution)/shard_map/move_out/pallas_call | solution.py:395
